TPU v7x, 32 devices: a whole 2x2x4 slice. The times are simulated.
32 devices in a mesh: snp: 8 (over y, x, core), prog: 4 (over z).
Axes of the slice: x: 2, y: 2, z: 4, core: 2. Of those that a mesh axis runs over, the one named last changes fastest.
Arguments:
- gene_score: bfloat16 [1024, 1024], P('snp', 'prog'), may hold values from 0 to 1
- link_gene: int32 [24576, 8], P('snp'), may hold values from 0 to 1023, as said below
- link_weight: bfloat16 [24576, 8], P('snp'), may hold values from 0.099609375 to 1
- ld_levels: bfloat16 [192, 5, 128, 128], P('snp'), may hold values from 0 to 1
- ld_scale: float32 [192, 5], P('snp'), may hold values from 0.2 to 1
- snp_weight: float32 [24576], P('snp'), may hold values from 0.25 to 6, as said below
- trait_z: bfloat16 [24576, 4096], P('snp', 'prog'), may hold values from -6 to 6
- jk_unit: int32 [8, 12], P('snp'), may hold values from 0 to 2, never falling along the last dimension, each value on 1 to 6 neighbouring positions
Outputs:
- delete_one: bfloat16 [24, 1024, 4096], P('snp', None, 'prog')
- block_estimate: bfloat16 [24, 1024, 4096], P('snp', None, 'prog')
Inputs may be any that keep to these rules, and one draw needn't show every extreme that they name: `link_gene`: A SNP of slab i names 8 distinct genes, all in gene blocks i - 1, i and i + 1 (block b holds genes b * 128 to (b + 1) * 128 - 1; blocks before the first and after the last don't exist). `snp_weight`: Positive. `jk_unit`: along each row the numbers never fall and each of the 3 numbers appears; a block holds at most 6 units, and some block of each row exactly that many.
All inputs are finite; a program needn't handle non-finite values.
Results may differ from a plain program's by a relative error of at most 0.012.
Values may be sent and summed in bfloat16 or wider, within the bound.
A program may use at most 192 MiB of HBM per device.

v0:
```python
import jax
import jax.numpy as jnp
from jax import lax
from jax.sharding import PartitionSpec as P

JK_DEV = 3


def padded_2(block, sides, width):
    for axis, dim in sides:
        count = lax.axis_size(axis)
        forward = [(i, i + 1) for i in range(count - 1)]
        backward = [(target, source) for source, target in forward]
        low = lax.ppermute(
            lax.slice_in_dim(block, block.shape[dim] - width, None, axis=dim), axis, forward
        )
        high = lax.ppermute(lax.slice_in_dim(block, 0, width, axis=dim), axis, backward)
        block = jnp.concatenate([low, block, high], axis=dim)
    return block


def annotate(gene_table, link_gene, link_weight, first_gene):
    local_gene = link_gene - first_gene
    table_rows = lax.broadcasted_iota(jnp.int32, (1, gene_table.shape[0]), 1)
    mixing = jnp.zeros((link_gene.shape[0], gene_table.shape[0]), jnp.float32)
    for link_slot in range(link_gene.shape[1]):
        strength = link_weight[:, link_slot : link_slot + 1].astype(jnp.float32)
        mixing = mixing + jnp.where(
            local_gene[:, link_slot : link_slot + 1] == table_rows, strength, 0.0
        )
    product = jnp.dot(mixing.astype(jnp.bfloat16), gene_table, preferred_element_type=jnp.float32)
    return product.astype(jnp.bfloat16)


def ld_scores(gene_table, link_gene, link_weight, ld_levels, ld_scale):
    rows_here = gene_table.shape[0]
    snp_rows = link_gene.shape[0]
    tile_rows = ld_levels.shape[2]
    band_count = ld_levels.shape[1]
    reach_rows = band_count // 2 * tile_rows
    padded_genes = padded_2(gene_table, (("snp", 0),), rows_here)
    first_gene = (lax.axis_index("snp") - 1) * rows_here
    annotation = annotate(padded_genes, link_gene, link_weight, first_gene)
    padded = padded_2(annotation, (("snp", 0),), reach_rows)
    tile_count = snp_rows // tile_rows
    columns = gene_table.shape[1]
    banded = jnp.zeros((tile_count, tile_rows, columns), jnp.float32)
    for offset in range(band_count):
        window = padded[offset * tile_rows : offset * tile_rows + snp_rows].reshape(
            tile_count, tile_rows, columns
        )
        levels = ld_levels[:, offset]
        product = jnp.einsum("nrt,ntp->nrp", levels, window, preferred_element_type=jnp.float32)
        banded = banded + ld_scale[:, offset][:, None, None] * product
    return banded.reshape(snp_rows, columns).astype(jnp.bfloat16)


def block_terms(weighted, trait_z, member):
    unit_count = member.shape[1]
    row_count = weighted.shape[0]
    unit_rows = row_count // unit_count
    row_member = jnp.repeat(member, unit_rows, axis=1).astype(jnp.bfloat16)
    masked = row_member[:, :, None] * weighted[None]
    return jnp.einsum("jsp,sk->jpk", masked, trait_z, preferred_element_type=jnp.float32)


def on_device(
    gene_score, link_gene, link_weight, ld_levels, ld_scale, snp_weight, trait_z, jk_unit
):
    unit_count = jk_unit.shape[1]
    member = (
        jk_unit[0][None, :] == lax.broadcasted_iota(jnp.int32, (JK_DEV, unit_count), 0)
    ).astype(jnp.float32)
    gene_table = lax.all_gather(gene_score, "prog", axis=1, tiled=True)
    scores = ld_scores(gene_table, link_gene, link_weight, ld_levels, ld_scale)
    columns = scores.shape[1]
    score_float = scores.astype(jnp.float32)
    weighted = (snp_weight[:, None] * score_float).astype(jnp.bfloat16)
    squares = (
        (snp_weight[:, None] * score_float * score_float)
        .reshape(unit_count, -1, columns)
        .sum(axis=1)
    )
    square_share = jnp.dot(member, squares, precision=lax.Precision.HIGHEST)
    crossed = block_terms(weighted, trait_z, member)
    summed, summed_sq = lax.psum((jnp.sum(crossed, axis=0), jnp.sum(square_share, axis=0)), "snp")
    estimate = (summed[None] - crossed) / jnp.sqrt(summed_sq[None] - square_share)[:, :, None]
    own_estimate = crossed / jnp.sqrt(square_share)[:, :, None]
    return (estimate.astype(jnp.bfloat16), own_estimate.astype(jnp.bfloat16))


def solution(mesh):
    placed = (
        P("snp", "prog"),
        P("snp", None),
        P("snp", None),
        P("snp", None, None, None),
        P("snp", None),
        P("snp"),
        P("snp", "prog"),
        P("snp", None),
    )
    return jax.shard_map(
        on_device,
        mesh=mesh,
        in_specs=placed,
        out_specs=(P("snp", None, "prog"), P("snp", None, "prog")),
        check_vma=False,
    )
```

profile of v0, /device:TPU:0, one launch (start us, length us, event | category | flops | bytes accessed | tf_op | source)
XLA Modules:
  0.0 260.7 jit_solution(13815285610389077264)
XLA Ops:
  7.2 0.0 all-reduce.2.cloned.1.call-start
  7.2 15.8 %all_gather.3 = bf16[128,1024]{1,0:T(8,128)(2,1)S(1)} all-gather(bf16[128,256]{1,0:T(8,128)(2,1)} %param.8), channel_id=1, replica_groups=mesh['snp'=8,'prog'=4] {'prog'}, dimensions={1}, use_global_device_ids=true | all-gather | bytes 327680 | tf_op jit(solution)/shard_map/all_gather | solution.py:74
  23.0 1.3 collective-permute-start
  24.4 1.3 collective-permute-start.1
  25.7 0.9 broadcast_subtract_fusion
  26.6 0.1 fusion.51
  26.6 1.3 slice_convert_fusion.7
  27.9 0.7 convert_convert_fusion
  28.6 0.1 broadcast_bitcast_fusion
  28.7 0.9 slice_bitcast_fusion.4
  29.6 0.0 collective-permute-done
  29.6 0.0 collective-permute-done.1
  29.6 0.1 fusion.64
  29.7 12.3 %convolution_convert_fusion = bf16[3072,1024]{1,0:T(8,128)(2,1)S(1)} fusion(f32[3072]{0:T(1024)S(1)} %bitcast.107, s32[3072]{0:T(1024)S(1)} %bitcast.94, f32[3072]{0:T(1024)S(1)} %bitcast.108, s32[3072]{0:T(1024)S(1)} %bitcast.95, f32[3072]{0:T(1024)S(1)} %bitcast.102, s32[3072]{0:T(1024)S(1)} %bitcast.96, f32[3072]{0:T(1024)S(1)} %bitcast.103, ...), kind=kOutput, calls=%fused_computation.21 | convolution fusion | flops 2447376384 | bytes 7274496 | tf_op jit(solution)/shard_map/dot_general | solution.py:31
  41.9 0.1 fusion.50
  42.0 6.7 %collective-permute-start.2 = (bf16[256,1024]{1,0:T(8,128)(2,1)S(1)}, bf16[256,1024]{1,0:T(8,128)(2,1)S(1)}, u32[]{:S(2)}, u32[]{:S(2)}) collective-permute-start(bf16[256,1024]{1,0:T(8,128)(2,1)S(1)} %get-tuple-element.10), channel_id=1, source_target_pairs={{0,4},{4,8},{8,12},{12,16},{16,20},{20,24},{24,28},{1,5},{5,9},{9,... | collective-permute-start | bytes 1572872 | tf_op jit(solution)/shard_map/ppermute | solution.py:14
  48.7 1.3 collective-permute-start.3
  50.0 2.9 %fusion.35 = f32[24,1024,128]{1,2,0:T(8,128)S(1)} fusion(bf16[24,128,1024]{2,1,0:T(8,128)(2,1)S(1)} %bitcast.82, bf16[24,5,128,128]{3,2,1,0:T(8,128)(2,1)} %param.11), kind=kOutput, calls=%fused_computation.56 | convolution fusion | flops 805306368 | bytes 19660800 | tf_op jit(solution)/shard_map/nrt,ntp->nrp/dot_general | solution.py:53
  52.9 0.0 collective-permute-done.2
  52.9 0.0 collective-permute-done.3
  52.9 8.8 %pad_maximum_fusion = (bf16[3072,1024]{1,0:T(8,128)(2,1)}, bf16[3072,1024]{1,0:T(8,128)(2,1)}, bf16[3072,1024]{1,0:T(8,128)(2,1)}, bf16[3072,1024]{1,0:T(8,128)(2,1)}) fusion(bf16[256,1024]{1,0:T(8,128)(2,1)S(1)} %collective-permute-done.3, bf16[3072,1024]{1,0:T(8,128)(2,1)S(1)} %convolution_convert_fusion, bf16[256,1024]{1,0:T(8,128)(2,1)S(1)} %collective-permute-done.2), kind=kLoop, calls=%fused_computation.18 | loop fusion | flops 50331648 | bytes 32505856 | tf_op jit(solution)/shard_map/concatenate | solution.py:18
  61.7 0.0 slice-start.2
  61.7 0.0 slice-start.3
  61.7 0.0 copy-start
  61.7 9.5 %fusion.33 = f32[24,1024,128]{1,2,0:T(8,128)} fusion(bf16[24,128,1024]{2,1,0:T(8,128)(2,1)} %bitcast.89, bf16[24,5,128,128]{3,2,1,0:T(8,128)(2,1)} %param.11), kind=kOutput, calls=%fused_computation.54 | convolution fusion | flops 805306368 | bytes 19660800 | tf_op jit(solution)/shard_map/nrt,ntp->nrp/dot_general | solution.py:53
  71.2 0.0 slice-start
  71.3 0.0 slice-done.2
  71.3 0.0 slice-done.3
  71.3 0.0 copy-done
  71.3 0.0 slice-start.1
  71.3 6.3 %fusion.37 = f32[24,1024,128]{1,2,0:T(8,128)} fusion(bf16[24,128,1024]{2,1,0:T(8,128)(2,1)S(1)} %bitcast.88, bf16[24,5,128,128]{3,2,1,0:T(8,128)(2,1)S(1)} %copy-done), kind=kOutput, calls=%fused_computation.58 | convolution fusion | flops 805306368 | bytes 19660800 | tf_op jit(solution)/shard_map/nrt,ntp->nrp/dot_general | solution.py:53
  77.6 0.0 slice-done
  77.6 0.0 slice-done.1
  77.6 0.0 copy-start.1
  77.6 6.4 %fusion.39 = f32[24,1024,128]{1,2,0:T(8,128)} fusion(bf16[24,128,1024]{2,1,0:T(8,128)(2,1)S(1)} %bitcast.85, bf16[24,5,128,128]{3,2,1,0:T(8,128)(2,1)S(1)} %copy-done), kind=kOutput, calls=%fused_computation.60 | convolution fusion | flops 805306368 | bytes 19660800 | tf_op jit(solution)/shard_map/nrt,ntp->nrp/dot_general | solution.py:53
  84.0 0.0 copy-done.1
  84.0 20.7 %fusion.2 = (f32[24,1024]{1,0:T(8,128)S(1)}, f32[24,1024,128]{1,2,0:T(8,128)}) fusion(f32[24,128]{1,0:T(8,128)S(1)} %bitcast.91, bf16[24,128,1024]{2,1,0:T(8,128)(2,1)} %bitcast.90, bf16[24,5,128,128]{3,2,1,0:T(8,128)(2,1)} %param.11, f32[24]{0:T(128)S(1)} %get-tuple-element.33, f32[24,1024,128]{1,2,0:T(8,128)} %fusion.33, f32[24]{0:T(128)S(1)} %get-tuple-element.34, ...), kind=kOutput, calls=%fused_computation.3 | convolution fusion | flops 849321984 | bytes 70103520 | tf_op jit(solution)/shard_map/nrt,ntp->nrp/dot_general | solution.py:53
  104.6 8.0 %fusion.3 = bf16[3072,1024]{1,0:T(8,128)(2,1)} fusion(f32[24,1024,128]{1,2,0:T(8,128)} %get-tuple-element.36, f32[3072]{0:T(1024)S(1)} %copy-done.1), kind=kLoop, calls=%fused_computation.5 | loop fusion | flops 6291456 | bytes 18886656 | tf_op jit(solution)/shard_map/convert_element_type | solution.py:78
  112.6 8.6 %copy.21 = bf16[3072,1024]{0,1:T(8,128)(2,1)} copy(bf16[3072,1024]{1,0:T(8,128)(2,1)} %fusion.3) | data formatting | bytes 12582912 | tf_op jit(solution)/shard_map/convert_element_type | solution.py:78
  121.2 29.3 %fusion.54 = (f32[1024,1024]{1,0:T(8,128)}, f32[3,1024,1024]{2,1,0:T(8,128)}) fusion(bf16[3072,1024]{1,0:T(8,128)(2,1)} %param.14, bf16[3072,1024]{0,1:T(8,128)(2,1)} %copy.21, bf16[3,3072]{1,0:T(4,128)(2,1)S(1)} %bitcast.92), kind=kOutput, calls=%fused_computation.93 | convolution fusion | flops 19338887168 | bytes 29378560 | tf_op jit(solution)/shard_map/jsp,sk->jpk/dot_general | solution.py:64
  150.5 0.0 all-reduce.2.cloned.1.call-update
  150.5 0.1 reduce_sum.36
  150.6 0.1 reduce_sum.37
  150.7 0.0 copy-done.2
  150.7 0.2 fusion.53
  150.9 21.9 %psum.15 = f32[1024]{0:T(1024)S(1)} all-reduce(f32[1024]{0:T(1024)S(1)} %get-tuple-element.37), channel_id=1, replica_groups=mesh['snp'=8,'prog'=4] {'snp'}, use_global_device_ids=true, to_apply=%region_5.6 | all-reduce | flops 1024 | bytes 8192 | tf_op jit(solution)/shard_map/psum | solution.py:86
  172.8 68.2 %all-reduce.2.cloned.1.call-done = f32[1024,1024]{1,0:T(8,128)} async-done(((f32[1024,1024]{1,0:T(8,128)}), f32[1024,1024]{1,0:T(8,128)}) %all-reduce.2.cloned.1.call-update) | async-done | bytes 4194320 | tf_op jit(solution)/shard_map/psum | solution.py:86
  241.0 12.8 %divide_convert_fusion = (bf16[3,1024,1024]{2,1,0:T(8,128)(2,1)}, bf16[3,1024,1024]{2,1,0:T(8,128)(2,1)}) fusion(f32[3,1024,1024]{2,1,0:T(8,128)} %get-tuple-element.40, f32[3,1024]{1,0:T(4,128)S(1)} %get-tuple-element.28, f32[3,1024]{1,0:T(4,128)S(1)} %get-tuple-element.29, f32[1024,1024]{1,0:T(8,128)} %all-reduce.2.cloned.1.call-done), kind=kLoop, calls=%fused_computation.7 | loop fusion | flops 15728640 | bytes 29384704 | tf_op jit(solution)/shard_map/convert_element_type | solution.py:89
  (5 shorter events, 0.0 us)
Async XLA Ops:
  7.2 233.9 %all-reduce.2.cloned.1.call-start = ((), (), s32[]{:S(2)}) async-start(), calls=%async_computation | async-start | bytes 8388608 | tf_op jit(solution)/shard_map/psum | solution.py:86
  23.0 6.5 %collective-permute-start = (bf16[128,1024]{1,0:T(8,128)(2,1)S(1)}, bf16[128,1024]{1,0:T(8,128)(2,1)S(1)}, u32[]{:S(2)}, u32[]{:S(2)}) collective-permute-start(bf16[128,1024]{1,0:T(8,128)(2,1)S(1)} %all_gather.3), channel_id=1, source_target_pairs={{0,4},{4,8},{8,12},{12,16},{16,20},{20,24},{24,28},{1,5},{5,9},{9,... | collective-permute-start | bytes 786440 | tf_op jit(solution)/shard_map/ppermute | solution.py:14
  24.4 5.2 %collective-permute-start.1 = (bf16[128,1024]{1,0:T(8,128)(2,1)S(1)}, bf16[128,1024]{1,0:T(8,128)(2,1)S(1)}, u32[]{:S(2)}, u32[]{:S(2)}) collective-permute-start(bf16[128,1024]{1,0:T(8,128)(2,1)S(1)} %all_gather.3), channel_id=1, source_target_pairs={{4,0},{8,4},{12,8},{16,12},{20,16},{24,20},{28,24},{5,1},{9,5},{13... | collective-permute-start | bytes 786440 | tf_op jit(solution)/shard_map/ppermute | solution.py:17
  42.0 10.9 %collective-permute-start.2 = (bf16[256,1024]{1,0:T(8,128)(2,1)S(1)}, bf16[256,1024]{1,0:T(8,128)(2,1)S(1)}, u32[]{:S(2)}, u32[]{:S(2)}) collective-permute-start(bf16[256,1024]{1,0:T(8,128)(2,1)S(1)} %get-tuple-element.10), channel_id=1, source_target_pairs={{0,4},{4,8},{8,12},{12,16},{16,20},{20,24},{24,28},{1,5},{5,9},{9,... | collective-permute-start | bytes 1572872 | tf_op jit(solution)/shard_map/ppermute | solution.py:14
  48.7 4.3 %collective-permute-start.3 = (bf16[256,1024]{1,0:T(8,128)(2,1)S(1)}, bf16[256,1024]{1,0:T(8,128)(2,1)S(1)}, u32[]{:S(2)}, u32[]{:S(2)}) collective-permute-start(bf16[256,1024]{1,0:T(8,128)(2,1)S(1)} %get-tuple-element.11), channel_id=1, source_target_pairs={{4,0},{8,4},{12,8},{16,12},{20,16},{24,20},{28,24},{5,1},{9,5},{13... | collective-permute-start | bytes 1572872 | tf_op jit(solution)/shard_map/ppermute | solution.py:17
  61.7 9.5 %slice-start.2 = ((s8[6291456]{0:T(1024)(128)(4,1)}), s8[4194304]{0:T(1024)(128)(4,1)S(1)}, s32[]{:S(2)}) async-start(s8[6291456]{0:T(1024)(128)(4,1)} %bitcast.86), calls=%async_computation.3 | async-start | bytes 8388608
  61.7 9.5 %slice-start.3 = ((s8[6291456]{0:T(1024)(128)(4,1)}), s8[2097152]{0:T(1024)(128)(4,1)S(1)}, s32[]{:S(2)}) async-start(s8[6291456]{0:T(1024)(128)(4,1)} %bitcast.86), calls=%async_computation.4 | async-start | bytes 4194304
  61.7 9.5 %copy-start = (bf16[24,5,128,128]{3,2,1,0:T(8,128)(2,1)S(1)}, bf16[24,5,128,128]{3,2,1,0:T(8,128)(2,1)}, u32[]{:S(2)}) copy-start(bf16[24,5,128,128]{3,2,1,0:T(8,128)(2,1)} %param.11) | copy-start | bytes 11796484
  71.2 6.3 %slice-start = ((s8[6291456]{0:T(1024)(128)(4,1)}), s8[4194304]{0:T(1024)(128)(4,1)S(1)}, s32[]{:S(2)}) async-start(s8[6291456]{0:T(1024)(128)(4,1)} %bitcast.83), calls=%async_computation.1 | async-start | bytes 8388608
  71.3 6.3 %slice-start.1 = ((s8[6291456]{0:T(1024)(128)(4,1)}), s8[2097152]{0:T(1024)(128)(4,1)S(1)}, s32[]{:S(2)}) async-start(s8[6291456]{0:T(1024)(128)(4,1)} %bitcast.83), calls=%async_computation.2 | async-start | bytes 4194304
  77.6 6.4 %copy-start.1 = (f32[3072]{0:T(1024)S(1)}, f32[3072]{0:T(1024)}, u32[]{:S(2)}) copy-start(f32[3072]{0:T(1024)} %param.13) | copy-start | bytes 36868
  121.2 29.5 %copy-start.2 = (s32[1,12]{1,0:T(1,128)S(1)}, s32[1,12]{1,0:T(1,128)}, u32[]{:S(2)}) copy-start(s32[1,12]{1,0:T(1,128)} %param.15) | copy-start | bytes 148
Sparse Core Ops, SparseCore 0:
  150.7 90.3 all-reduce.1
where the time goes:
time: 261 us
  matrix products  87.5 us (34%)
  waiting for transfers between devices  68.2 us (26%)
  blocking collectives  37.7 us (14%)
  other arithmetic  32.7 us (13%)
  between operations  14.2 us (5%)
  starting transfers between devices  10.6 us (4%)
  local copies, waits for them, and re-layouts  9.8 us (4%)
    psum x1, waiting for transfers between devices, on_device(): lax.psum((jnp.sum(crossed, axis=0), jnp.sum(square_share, axis=0)), 'snp')  68.2 us
    dot_general x5, matrix products, ld_scores(): jnp.einsum('nrt,ntp->nrp', levels, window, preferred_element_type=jnp.flo...  45.7 us
    dot_general x1, matrix products, block_terms(): jnp.einsum('jsp,sk->jpk', masked, trait_z, preferred_element_type=jnp.flo...  29.3 us
    psum x1, blocking collectives, on_device(): lax.psum((jnp.sum(crossed, axis=0), jnp.sum(square_share, axis=0)), 'snp')  21.9 us
    all_gather x1, blocking collectives, on_device(): gene_table = lax.all_gather(gene_score, 'prog', axis=1, tiled=True)  15.8 us
    convert_element_type x1, other arithmetic, on_device(): return (estimate.astype(jnp.bfloat16), own_estimate.astype(jnp.bfloat16))  12.8 us
    dot_general x1, matrix products, annotate(): jnp.dot(mixing.astype(jnp.bfloat16), gene_table, preferred_element_type=j...  12.3 us
    concatenate x1, other arithmetic, padded_2(): block = jnp.concatenate([low, block, high], axis=dim)  8.8 us
  transfers between devices with their start and end apart: 5, of which 1 were waited for; matrix products, arithmetic and copies ran while one was open for 3% of the time, Pallas kernels for 0%

commit v1 on v0

v1 whole, which is shorter than its diff:
```python
import functools

import jax
import jax.numpy as jnp
from jax import lax
from jax.experimental import pallas as pl
from jax.experimental.pallas import tpu as pltpu
from jax.sharding import PartitionSpec as P

JK_DEV = 3
MESH = pl.DeviceIdType.MESH
F32 = jnp.float32
BF16 = jnp.bfloat16
ROW_CHUNKS = 4


def nt_dot(a, b, **kw):
    return lax.dot_general(a, b, (((1,), (1,)), ((), ())), preferred_element_type=F32, **kw)


def gather_kernel(
    n, zn, reach, gene_ref, idx_ref, lw_ref, table, idx, lw, zs, zr, ns, nr, rs, rr, ls, lr
):
    i = lax.axis_index("snp")
    q = lax.axis_index("prog")
    odd = i % 2
    step = 2 * odd - 1
    rows, cols = gene_ref.shape
    snps = idx_ref.shape[1]
    mate = i - step
    near = i + step
    far = i - 2 * step
    has_near = (near >= 0) & (near < n)
    has_far = (far >= 0) & (far < n)
    mate_near = mate - step
    mate_has_near = (mate_near >= 0) & (mate_near < n)

    barrier = pltpu.get_barrier_semaphore()

    def greet(target):
        pl.semaphore_signal(barrier, inc=1, device_id=target, device_id_type=MESH)

    for o in range(1, zn):
        greet((i, (q + o) % zn))
    greet((mate, q))

    @pl.when(has_near)
    def _():
        greet((near, q))

    @pl.when(has_far)
    def _():
        greet((far, q))

    far_from = i + 2 * step
    has_far_from = (far_from >= 0) & (far_from < n)

    @pl.when(has_far_from)
    def _():
        greet((far_from, q))

    own_rows = pl.ds(pl.multiple_of(q * cols, cols), cols)
    table[own_rows, 2 * rows : 3 * rows] = gene_ref[...].T
    idx[:, reach : reach + snps] = idx_ref[...]
    lw[:, reach : reach + snps] = lw_ref[...]

    def zero(slot):
        table[:, slot * rows : (slot + 1) * rows] = jnp.zeros((table.shape[0], rows), BF16)

    @pl.when(i < 2)
    def _():
        zero(0)

    @pl.when(i < 1)
    def _():
        zero(1)
        idx[:, :reach] = jnp.zeros((idx.shape[0], reach), jnp.int32)
        lw[:, :reach] = jnp.zeros((lw.shape[0], reach), F32)

    @pl.when(i > n - 2)
    def _():
        zero(3)
        idx[:, reach + snps :] = jnp.zeros((idx.shape[0], reach), jnp.int32)
        lw[:, reach + snps :] = jnp.zeros((lw.shape[0], reach), F32)

    @pl.when(i > n - 3)
    def _():
        zero(4)

    peers = zn
    for there in (has_near, has_far, has_far_from):
        peers = peers + there.astype(jnp.int32)
    pl.semaphore_wait(barrier, peers)

    def piece(slot, z):
        return table.at[
            pl.ds(pl.multiple_of(z * cols, cols), cols),
            pl.ds(pl.multiple_of(slot * rows, rows), rows),
        ]

    def z_copy(o):
        return pltpu.make_async_remote_copy(
            src_ref=piece(2, q),
            dst_ref=piece(2, q),
            send_sem=zs.at[o - 1],
            recv_sem=zr.at[o - 1],
            device_id=(i, (q + o) % zn),
            device_id_type=MESH,
        )

    def own_copy(kind, o):
        z = (q - o + zn) % zn
        target = (mate, near, far)[kind]
        return pltpu.make_async_remote_copy(
            src_ref=piece(2, z),
            dst_ref=piece(i - target + 2, z),
            send_sem=ns.at[kind, o],
            recv_sem=nr.at[kind, o],
            device_id=(target, q),
            device_id_type=MESH,
        )

    def own_arrive(kind, o):
        z = (q - o + zn) % zn
        source = (mate, near, far_from)[kind]
        return pltpu.make_async_remote_copy(
            src_ref=piece(2, z),
            dst_ref=piece(source - i + 2, z),
            send_sem=ns.at[kind, o],
            recv_sem=nr.at[kind, o],
            device_id=(mate, q),
            device_id_type=MESH,
        )

    def relay(o):
        z = (q - o + zn) % zn
        return pltpu.make_async_remote_copy(
            src_ref=piece(near - i + 2, z),
            dst_ref=piece(near - mate + 2, z),
            send_sem=rs.at[o],
            recv_sem=rr.at[o],
            device_id=(mate, q),
            device_id_type=MESH,
        )

    def relay_arrive(o):
        z = (q - o + zn) % zn
        return pltpu.make_async_remote_copy(
            src_ref=piece(2, z),
            dst_ref=piece(mate_near - i + 2, z),
            send_sem=rs.at[o],
            recv_sem=rr.at[o],
            device_id=(mate, q),
            device_id_type=MESH,
        )

    def link_copy(which, up):
        ref = (idx, lw)[which]
        src = pl.ds(snps if up else reach, reach)
        dst = pl.ds(0 if up else reach + snps, reach)
        return pltpu.make_async_remote_copy(
            src_ref=ref.at[:, src],
            dst_ref=ref.at[:, dst],
            send_sem=ls.at[which, up],
            recv_sem=lr.at[which, up],
            device_id=(i + 1 if up else i - 1, q),
            device_id_type=MESH,
        )

    for o in range(1, zn):
        z_copy(o).start()

    def send_own(o):
        own_copy(0, o).start()

        @pl.when(has_near)
        def _():
            own_copy(1, o).start()

        @pl.when(has_far)
        def _():
            own_copy(2, o).start()

    send_own(0)

    @pl.when(i < n - 1)
    def _():
        link_copy(0, 1).start()
        link_copy(1, 1).start()

    @pl.when(i > 0)
    def _():
        link_copy(0, 0).start()
        link_copy(1, 0).start()

    for o in range(1, zn):
        pltpu.make_async_remote_copy(
            src_ref=piece(2, q),
            dst_ref=piece(2, (q - o + zn) % zn),
            send_sem=zs.at[o - 1],
            recv_sem=zr.at[o - 1],
            device_id=(mate, q),
            device_id_type=MESH,
        ).wait_recv()
        send_own(o)

    @pl.when(has_near)
    def _():
        for o in range(zn):
            own_arrive(1, o).wait_recv()
            relay(o).start()

    for o in range(zn):
        own_arrive(0, o).wait_recv()

    @pl.when(has_far_from)
    def _():
        for o in range(zn):
            own_arrive(2, o).wait_recv()

    @pl.when(mate_has_near)
    def _():
        for o in range(zn):
            relay_arrive(o).wait_recv()

    @pl.when(i < n - 1)
    def _():
        for which in range(2):
            link_copy(which, 0).wait_recv()
            link_copy(which, 1).wait_send()

    @pl.when(i > 0)
    def _():
        for which in range(2):
            link_copy(which, 1).wait_recv()
            link_copy(which, 0).wait_send()

    for o in range(1, zn):
        z_copy(o).wait_send()
    for o in range(zn):
        own_copy(0, o).wait_send()

    @pl.when(has_near)
    def _():
        for o in range(zn):
            own_copy(1, o).wait_send()
            relay(o).wait_send()

    @pl.when(has_far)
    def _():
        for o in range(zn):
            own_copy(2, o).wait_send()


def score_kernel(
    band, jk_ref, scale_ref, table, idx, lw, levels, sw, out, sq, ann, square
):
    unit = pl.program_id(0)
    tile = levels.shape[2]
    rows = table.shape[1] // 5
    group = levels.shape[0]
    wide = group * tile
    chunks = ann.shape[1] // wide
    reach = band // 2 * tile
    span = 3 * rows

    def annotate(start, slot):
        at = pl.ds(pl.multiple_of(start, wide), wide)
        first = (lax.axis_index("snp") - 2 + slot) * rows
        local = idx[:, at] - first
        strength = lw[:, at]
        gene = lax.broadcasted_iota(jnp.int32, (span, wide), 0)
        mix = jnp.zeros((span, wide), F32)
        for link in range(idx.shape[0]):
            mix = jnp.where(
                local[link : link + 1] == gene, strength[link : link + 1], mix
            )
        ann[:, at] = jnp.dot(
            table[:, slot * rows : slot * rows + span],
            mix.astype(BF16),
            preferred_element_type=F32,
        ).astype(BF16)

    @pl.when(unit == 0)
    def _():
        square[...] = jnp.zeros_like(square)
        for start in range(0, reach, wide):
            annotate(start, 0)
            annotate(ann.shape[1] - reach + start, 2)

        @pl.loop(reach // wide, chunks - reach // wide)
        def _(c):
            annotate(c * wide, 1)

    blocks = []
    for g in range(group):
        parts = [jnp.zeros((tile, tile), BF16)] * g
        for d in range(band):
            s = scale_ref[unit * group + g, d]
            parts.append((levels[g, d].astype(F32) * s).astype(BF16))
        parts += [jnp.zeros((tile, tile), BF16)] * (group - 1 - g)
        blocks.append(jnp.concatenate(parts, axis=1))
    mixer = jnp.concatenate(blocks, axis=0)
    window = ann[:, pl.ds(pl.multiple_of(unit * wide, wide), mixer.shape[1])]
    score = nt_dot(window, mixer).astype(BF16).astype(F32)
    weighted = sw[...] * score
    out[...] = weighted.astype(BF16)
    part = weighted * score
    part = sum(part[:, a : a + 128] for a in range(0, wide, 128))
    j = jk_ref[0, unit]
    square[j] += part

    @pl.when(unit == pl.num_programs(0) - 1)
    def _():
        ones = jnp.ones((8, 128), F32)
        for j in range(JK_DEV):
            line = nt_dot(ones, square[j], precision=lax.Precision.HIGHEST)
            for r in range(sq.shape[1]):
                sq[j, r : r + 1, :] = line[0:1, r * 128 : (r + 1) * 128]


def cross_kernel(
    n, w_ref, z_ref, mask_ref, sq_ref, crossed, total, sq_total,
    acc, c_out, c_in, p_out, p_in, q_out, q_in,
    cs, cr, ps, pr, gs, gr, hs, hr, qs, qr,
):
    i = lax.axis_index("snp")
    z = lax.axis_index("prog")
    c = i % 2
    m = i // 2
    chips = n // 2
    mate = i + 1 - 2 * c
    chunks = ROW_CHUNKS
    rows = w_ref.shape[0] // chunks
    half = rows // 2
    own = half // chips
    half_s = w_ref.shape[1] // 2

    barrier = pltpu.get_barrier_semaphore()
    for o in range(1, n):
        pl.semaphore_signal(barrier, inc=1, device_id=((i + o) % n, z), device_id_type=MESH)
    q_out[...] = sq_ref[0] + sq_ref[1] + sq_ref[2]

    def remote(src, dst, s, r, device):
        return pltpu.make_async_remote_copy(
            src_ref=src, dst_ref=dst, send_sem=s, recv_sem=r,
            device_id=(device, z), device_id_type=MESH,
        )

    def sq_copy(o):
        return remote(q_out, q_in.at[o - 1], qs.at[o - 1], qr.at[o - 1], (i + o) % n)

    def core_copy(k):
        return remote(c_out.at[k], c_in.at[k], cs.at[k], cr.at[k], mate)

    def peer_copy(k, o):
        owner = (m + o) % chips
        return remote(
            p_out.at[k, pl.ds(pl.multiple_of(owner * own, own), own)],
            p_in.at[k, o - 1], ps.at[k, o - 1], pr.at[k, o - 1], owner * 2 + c,
        )

    def place(k, core, chip):
        return pl.ds(pl.multiple_of(k * rows + core * half + chip * own, own), own)

    def gather_copy(k, o):
        at = total.at[place(k, c, m)]
        return remote(at, at, gs.at[k, o - 1], gr.at[k, o - 1], (m + o) % chips * 2 + c)

    def gather_arrive(k, o):
        at = total.at[place(k, c, (m + chips - o) % chips)]
        return remote(at, at, gs.at[k, o - 1], gr.at[k, o - 1], mate)

    def half_copy(k, core):
        at = total.at[pl.ds(pl.multiple_of(k * rows + core * half, half), half)]
        return remote(at, at, hs.at[k], hr.at[k], mate)

    def compute(k):
        at = slice(k * rows, (k + 1) * rows)
        acc[at, :] = jnp.dot(w_ref[at, :], z_ref[...], preferred_element_type=F32)
        away = pl.ds(pl.multiple_of(k * rows + (1 - c) * half, half), half)
        c_out[k] = acc[away, :].astype(BF16)

    def after_core(k):
        core_copy(k).wait_recv()
        home = pl.ds(pl.multiple_of(k * rows + c * half, half), half)
        p_out[k] = (acc[home, :] + c_in[k].astype(F32)).astype(BF16)
        for o in range(1, chips):
            peer_copy(k, o).start()

    def after_peers(k):
        for o in range(1, chips):
            peer_copy(k, o).wait_recv()
        s = p_out[k, pl.ds(pl.multiple_of(m * own, own), own)].astype(F32)
        for o in range(1, chips):
            s = s + p_in[k, o - 1].astype(F32)
        total[place(k, c, m), :] = s.astype(BF16)
        for o in range(1, chips):
            gather_copy(k, o).start()

    def after_gather(k):
        for o in range(1, chips):
            gather_arrive(k, o).wait_recv()
        half_copy(k, c).start()

    def split(k):
        at = slice(k * rows, (k + 1) * rows)
        first = jnp.dot(
            w_ref[at, :half_s] * mask_ref[0:1, :half_s], z_ref[:half_s, :],
            preferred_element_type=F32,
        )
        last = jnp.dot(
            w_ref[at, half_s:] * mask_ref[1:2, half_s:], z_ref[half_s:, :],
            preferred_element_type=F32,
        )
        crossed[0, at, :] = first.astype(BF16)
        crossed[2, at, :] = last.astype(BF16)
        crossed[1, at, :] = (acc[at, :] - first - last).astype(BF16)

    compute(0)
    pl.semaphore_wait(barrier, n - 1)
    core_copy(0).start()
    for o in range(1, n):
        sq_copy(o).start()
    for k in range(1, chunks):
        compute(k)
        core_copy(k).start()
        after_core(k - 1)
    split(0)
    after_core(chunks - 1)
    after_peers(0)
    for k in range(1, chunks):
        split(k)
        after_peers(k)
        after_gather(k - 1)
    after_gather(chunks - 1)
    s = q_out[...]
    for o in range(1, n):
        sq_copy(o).wait_recv()
        s = s + q_in[o - 1]
    sq_total[...] = s
    for o in range(1, n):
        sq_copy(o).wait_send()
    for k in range(chunks):
        half_copy(k, 1 - c).wait_recv()
        half_copy(k, c).wait_send()
        core_copy(k).wait_send()
        for o in range(1, chips):
            peer_copy(k, o).wait_send()
            gather_copy(k, o).wait_send()


def estimate_kernel(crossed, total, leave, keep, delete_one, own):
    whole = total[...].astype(F32)
    for j in range(JK_DEV):
        part = crossed[j].astype(F32)
        delete_one[j] = ((whole - part) * leave[j]).astype(BF16)
        own[j] = (part * keep[j]).astype(BF16)


def on_device(
    n, zn, gene_score, link_gene, link_weight, ld_levels, ld_scale, snp_weight, trait_z, jk_unit
):
    unit_count = jk_unit.shape[1]
    snps, links = link_gene.shape
    tiles, band, tile, _ = ld_levels.shape
    reach = band // 2 * tile
    rows, cols = gene_score.shape
    programs = cols * zn
    traits = trait_z.shape[1]
    wide = snps // unit_count
    group = wide // tile
    vmem = pl.BlockSpec(memory_space=pltpu.VMEM)
    smem = pl.BlockSpec(memory_space=pltpu.SMEM)
    dma = pltpu.SemaphoreType.DMA
    limit = 60 * 1024 * 1024

    table, idx, lw = pl.pallas_call(
        functools.partial(gather_kernel, n, zn, reach),
        out_shape=(
            jax.ShapeDtypeStruct((programs, 5 * rows), BF16),
            jax.ShapeDtypeStruct((links, snps + 2 * reach), jnp.int32),
            jax.ShapeDtypeStruct((links, snps + 2 * reach), F32),
        ),
        in_specs=[vmem] * 3,
        out_specs=(vmem,) * 3,
        scratch_shapes=[
            dma((zn - 1,)), dma((zn - 1,)), dma((3, zn)), dma((3, zn)),
            dma((zn,)), dma((zn,)), dma((2, 2)), dma((2, 2)),
        ],
        compiler_params=pltpu.CompilerParams(collective_id=0, has_side_effects=True),
        name="gather_genes",
    )(gene_score, link_gene.T, link_weight.T.astype(F32))

    weighted, square = pl.pallas_call(
        functools.partial(score_kernel, band),
        grid=(unit_count,),
        out_shape=(
            jax.ShapeDtypeStruct((programs, snps), BF16),
            jax.ShapeDtypeStruct((JK_DEV, programs // 128, 128), F32),
        ),
        in_specs=[
            smem,
            smem,
            vmem,
            vmem,
            vmem,
            pl.BlockSpec((group, band, tile, tile), lambda u: (u, 0, 0, 0)),
            pl.BlockSpec((1, wide), lambda u: (0, u)),
        ],
        out_specs=(
            pl.BlockSpec((programs, wide), lambda u: (0, u)),
            pl.BlockSpec((JK_DEV, programs // 128, 128), lambda u: (0, 0, 0)),
        ),
        scratch_shapes=[
            pltpu.VMEM((programs, snps + 2 * reach), BF16),
            pltpu.VMEM((JK_DEV, programs, 128), F32),
        ],
        compiler_params=pltpu.CompilerParams(vmem_limit_bytes=limit),
        name="ld_scores",
    )(jk_unit, ld_scale, table, idx, lw, ld_levels, snp_weight[None])

    ends = jnp.array([0, JK_DEV - 1], jnp.int32)
    mask = jnp.repeat(jk_unit[0][None] == ends[:, None], wide, axis=1).astype(BF16)
    mask = jnp.pad(mask, ((0, 14), (0, 0)))

    k = ROW_CHUNKS
    half = programs // k // 2
    chips = n // 2
    crossed, total, sq_total = pl.pallas_call(
        functools.partial(cross_kernel, n),
        out_shape=(
            jax.ShapeDtypeStruct((JK_DEV, programs, traits), BF16),
            jax.ShapeDtypeStruct((programs, traits), BF16),
            jax.ShapeDtypeStruct((programs // 128, 128), F32),
        ),
        in_specs=[vmem] * 4,
        out_specs=(vmem,) * 3,
        scratch_shapes=[
            pltpu.VMEM((programs, traits), F32),
            pltpu.VMEM((k, half, traits), BF16),
            pltpu.VMEM((k, half, traits), BF16),
            pltpu.VMEM((k, half, traits), BF16),
            pltpu.VMEM((k, chips - 1, half // chips, traits), BF16),
            pltpu.VMEM((programs // 128, 128), F32),
            pltpu.VMEM((n - 1, programs // 128, 128), F32),
            dma((k,)), dma((k,)),
            dma((k, chips - 1)), dma((k, chips - 1)),
            dma((k, chips - 1)), dma((k, chips - 1)),
            dma((k,)), dma((k,)),
            dma((n - 1,)), dma((n - 1,)),
        ],
        compiler_params=pltpu.CompilerParams(
            collective_id=1, has_side_effects=True, vmem_limit_bytes=limit
        ),
        name="cross_total",
    )(weighted, trait_z, mask, square)

    keep = (1.0 / jnp.sqrt(square)).reshape(JK_DEV, programs, 1)
    leave = (1.0 / jnp.sqrt(sq_total[None] - square)).reshape(JK_DEV, programs, 1)
    block = programs // 8
    whole = pl.BlockSpec((JK_DEV, block, traits), lambda p: (0, p, 0))
    column = pl.BlockSpec((JK_DEV, block, 1), lambda p: (0, p, 0))
    return pl.pallas_call(
        estimate_kernel,
        grid=(programs // block,),
        out_shape=(jax.ShapeDtypeStruct((JK_DEV, programs, traits), BF16),) * 2,
        in_specs=[whole, pl.BlockSpec((block, traits), lambda p: (p, 0)), column, column],
        out_specs=(whole, whole),
        compiler_params=pltpu.CompilerParams(vmem_limit_bytes=limit),
        name="estimates",
    )(crossed, total, leave, keep)


def solution(mesh):
    placed = (
        P("snp", "prog"),
        P("snp", None),
        P("snp", None),
        P("snp", None, None, None),
        P("snp", None),
        P("snp"),
        P("snp", "prog"),
        P("snp", None),
    )
    return jax.shard_map(
        functools.partial(on_device, mesh.shape["snp"], mesh.shape["prog"]),
        mesh=mesh,
        in_specs=placed,
        out_specs=(P("snp", None, "prog"), P("snp", None, "prog")),
        check_vma=False,
    )
```

time: 261 us -> 109 us (0.42)
  Pallas kernels: 0 us -> 97.1 us
  matrix products: 87.5 us -> 0 us
  waiting for transfers between devices: 68.2 us -> 0 us
  blocking collectives: 37.7 us -> 0 us
  other arithmetic: 32.7 us -> 2.87 us
  between operations: 14.2 us -> 0.67 us
  starting transfers between devices: 10.6 us -> 0 us
    pallas_call x0 -> x4, Pallas kernels: none -> 97.1 us  [the longest x1 39.8 us: on_device(): pl.pallas_call(functools.partial(cross_kernel, n), out_shape=(jax.ShapeDt...]
    dot_general x8 -> x0, matrix products: 87.5 us -> none  [the longest x5 45.7 us: ld_scores(): jnp.einsum('nrt,ntp->nrp', levels, window, preferred_element_type=jnp.flo...]
    psum x1 -> x0, waiting for transfers between devices: 68.2 us -> none  [on_device(): lax.psum((jnp.sum(crossed, axis=0), jnp.sum(square_share, axis=0)), 'snp')]
    psum x1 -> x0, blocking collectives: 21.9 us -> none  [on_device(): lax.psum((jnp.sum(crossed, axis=0), jnp.sum(square_share, axis=0)), 'snp')]
    convert_element_type x3 -> x2, other arithmetic: 21.5 us -> 2.17 us  [the longest x1 1.45 us: on_device(): link_weight.T.astype(F32)]
    all_gather x1 -> x0, blocking collectives: 15.8 us -> none  [on_device(): gene_table = lax.all_gather(gene_score, 'prog', axis=1, tiled=True)]
    ppermute x4 -> x0, starting transfers between devices: 10.5 us -> none  [the longest x2 7.95 us: padded_2(): lax.ppermute(lax.slice_in_dim(block, block.shape[dim] - width, None, axis...]
    concatenate x1 -> x0, other arithmetic: 8.8 us -> none  [padded_2(): block = jnp.concatenate([low, block, high], axis=dim)]
  transfers between devices with their start and end apart: 5 -> 0, of which waited for: 1 -> 0; matrix products, arithmetic and copies ran while one was open for 3% -> 0% of each run, Pallas kernels for 0% -> 0%
where the time goes in v1:
time: 109 us; the launch traced here: 108 us
  Pallas kernels  97.1 us (89%)
  local copies, waits for them, and re-layouts  7.3 us (7%)
  other arithmetic  2.87 us (3%)
    pallas_call x1, Pallas kernels, on_device(): pl.pallas_call(functools.partial(cross_kernel, n), out_shape=(jax.ShapeDt...  39.8 us
    pallas_call x1, Pallas kernels, on_device(): pl.pallas_call(functools.partial(score_kernel, band), grid=(unit_count,),...  23.9 us
    pallas_call x1, Pallas kernels, on_device(): pl.pallas_call(functools.partial(gather_kernel, n, zn, reach), out_shape=...  21.7 us
    pallas_call x1, Pallas kernels, on_device(): pl.pallas_call(estimate_kernel, grid=(programs // block,), out_shape=(jax...  11.7 us
    reshape x1, local copies, waits for them, and re-layouts, on_device(): (1.0 / jnp.sqrt(sq_total[None] - square)).reshape(JK_DEV, programs, 1)  2.64 us
    reshape x1, local copies, waits for them, and re-layouts, on_device(): keep = (1.0 / jnp.sqrt(square)).reshape(JK_DEV, programs, 1)  2.55 us

profile of v1, /device:TPU:0, one launch (start us, length us, event | category | flops | bytes accessed | tf_op | source)
XLA Modules:
  0.0 107.9 jit_solution(10700694676875063050)
XLA Ops:
  0.6 0.7 compare_convert_fusion
  1.4 1.4 %copy.12.scale_ref = f32[24,5]{1,0:T(8,128)} copy(f32[24,5]{0,1:T(8,128)} %param.13) | data formatting | bytes 960 | tf_op args[4]
  2.7 0.1 broadcast_bitcast_fusion
  2.8 0.7 pad.4.mask_ref
  3.5 1.4 %convert_bitcast_fusion.lw_ref = f32[8,3072]{1,0:T(8,128)} fusion(bf16[3072,8]{0,1:T(8,128)(2,1)} %param.11), kind=kLoop, calls=%fused_computation | loop fusion | flops 24576 | bytes 147456 | tf_op jit(solution)/shard_map/convert_element_type | solution.py:493
  4.9 21.7 %gather_genes.1 = (bf16[1024,640]{1,0:T(8,128)(2,1)}, s32[8,3584]{1,0:T(8,128)}, f32[8,3584]{1,0:T(8,128)}) custom-call(bf16[128,256]{1,0:T(8,128)(2,1)} %gene_ref.1, s32[8,3072]{1,0:T(8,128)} %bitcast.8, f32[8,3072]{1,0:T(8,128)} %convert_bitcast_fusion.lw_ref), custom_call_target="tpu_custom_call" | custom-call | tf_op jit(solution)/shard_map/gather_genes/pallas_call | solution.py:478
  26.6 23.9 %ld_scores.1 = (bf16[1024,3072]{1,0:T(8,128)(2,1)}, f32[3,8,128]{2,1,0:T(8,128)}) custom-call(s32[1,12]{1,0:T(1,128)} %jk_ref.1, f32[24,5]{1,0:T(8,128)} %copy.12.scale_ref, bf16[1024,640]{1,0:T(8,128)(2,1)} %get-tuple-element.10.table, s32[8,3584]{1,0:T(8,128)} %get-tuple-element.11.idx, f32[8,3584]{1,0:T(8,128)} %get-tuple-element.12.lw, ...), custom_call_target="tpu_custom_call" | custom-call | tf_op jit(solution)/shard_map/ld_scores/pallas_call | solution.py:495
  50.5 0.0 copy-start
  50.5 39.8 %cross_total.1 = (bf16[3,1024,1024]{2,1,0:T(8,128)(2,1)}, bf16[1024,1024]{1,0:T(8,128)(2,1)}, f32[8,128]{1,0:T(8,128)}) custom-call(bf16[1024,3072]{1,0:T(8,128)(2,1)} %get-tuple-element.13.w_ref, bf16[3072,1024]{1,0:T(8,128)(2,1)} %z_ref.1, bf16[16,3072]{1,0:T(8,128)(2,1)} %pad.4.mask_ref, f32[3,8,128]{2,1,0:T(8,128)} %get-tuple-element.14.sq_ref), custom_call_target="tpu_custom_call" | custom-call | tf_op jit(solution)/shard_map/cross_total/pallas_call | solution.py:530
  90.3 0.0 copy-done
  90.3 0.7 fusion
  91.0 2.6 %reshape.17.keep = f32[3,1024,1]{2,1,0:T(8,128)} reshape(f32[3,8,128]{2,1,0:T(8,128)S(1)} %get-tuple-element.18) | data formatting | bytes 24576 | tf_op jit(solution)/shard_map/reshape | solution.py:559
  93.6 2.6 %reshape.16.leave = f32[3,1024,1]{2,1,0:T(8,128)} reshape(f32[3,8,128]{2,1,0:T(8,128)S(1)} %get-tuple-element.19) | data formatting | bytes 24576 | tf_op jit(solution)/shard_map/reshape | solution.py:560
  96.2 11.7 %estimates.1 = (bf16[3,1024,1024]{2,1,0:T(8,128)(2,1)}, bf16[3,1024,1024]{2,1,0:T(8,128)(2,1)}) custom-call(bf16[3,1024,1024]{2,1,0:T(8,128)(2,1)} %get-tuple-element.15.crossed, bf16[1024,1024]{1,0:T(8,128)(2,1)} %get-tuple-element.16.total, f32[3,1024,1]{2,1,0:T(8,128)} %reshape.16.leave, f32[3,1024,1]{2,1,0:T(8,128)} %reshape.17.keep), custom_call_target="tpu_custom_call" | custom-call | tf_op jit(solution)/shard_map/estimates/pallas_call | solution.py:564
  (2 shorter events, 0.0 us)
Async XLA Ops:
  50.5 39.8 %copy-start = (f32[3,8,128]{2,1,0:T(8,128)S(1)}, f32[3,8,128]{2,1,0:T(8,128)}, u32[]{:S(2)}) copy-start(f32[3,8,128]{2,1,0:T(8,128)} %get-tuple-element.14.sq_ref) | copy-start | bytes 36868

commit v2 on v1

--- a/solution.py
+++ b/solution.py
@@ -18,8 +18,16 @@
     return lax.dot_general(a, b, (((1,), (1,)), ((), ())), preferred_element_type=F32, **kw)
 
 
+def one_hot(local, strength, span):
+    gene = lax.broadcasted_iota(jnp.int32, (span, local.shape[1]), 0)
+    mix = jnp.zeros(gene.shape, F32)
+    for link in range(local.shape[0]):
+        mix = jnp.where(local[link : link + 1] == gene, strength[link : link + 1], mix)
+    return mix.astype(BF16)
+
+
 def gather_kernel(
-    n, zn, reach, gene_ref, idx_ref, lw_ref, table, idx, lw, zs, zr, ns, nr, rs, rr, ls, lr
+    n, zn, reach, wide, gene_ref, idx_ref, lw_ref, table, idx, lw, mix, zs, zr, ns, nr, rs, rr, ls, lr
 ):
     i = lax.axis_index("snp")
     q = lax.axis_index("prog")
@@ -62,7 +70,7 @@
     own_rows = pl.ds(pl.multiple_of(q * cols, cols), cols)
     table[own_rows, 2 * rows : 3 * rows] = gene_ref[...].T
     idx[:, reach : reach + snps] = idx_ref[...]
-    lw[:, reach : reach + snps] = lw_ref[...]
+    lw[:, reach : reach + snps] = lw_ref[...].astype(F32)
 
     def zero(slot):
         table[:, slot * rows : (slot + 1) * rows] = jnp.zeros((table.shape[0], rows), BF16)
@@ -167,6 +175,15 @@
             device_id_type=MESH,
         )
 
+    chunks = snps // wide
+
+    def build(lo, hi):
+        @pl.loop(lo, hi)
+        def _(c):
+            at = pl.ds(pl.multiple_of(c * wide, wide), wide)
+            inner = pl.ds(pl.multiple_of(c * wide + reach, wide), wide)
+            mix[:, at] = one_hot(idx[:, inner] - (i - 1) * rows, lw[:, inner], 3 * rows)
+
     for o in range(1, zn):
         z_copy(o).start()
 
@@ -194,6 +211,7 @@
         link_copy(1, 0).start()
 
     for o in range(1, zn):
+        build((o - 1) * chunks // zn, o * chunks // zn)
         pltpu.make_async_remote_copy(
             src_ref=piece(2, q),
             dst_ref=piece(2, (q - o + zn) % zn),
@@ -204,6 +222,8 @@
         ).wait_recv()
         send_own(o)
 
+    build((zn - 1) * chunks // zn, chunks)
+
     @pl.when(has_near)
     def _():
         for o in range(zn):
@@ -253,31 +273,22 @@
 
 
 def score_kernel(
-    band, jk_ref, scale_ref, table, idx, lw, levels, sw, out, sq, ann, square
+    band, jk_ref, scale_ref, table, idx, lw, mix, levels, sw, out, sq, mask, ann, square
 ):
     unit = pl.program_id(0)
     tile = levels.shape[2]
     rows = table.shape[1] // 5
     group = levels.shape[0]
     wide = group * tile
-    chunks = ann.shape[1] // wide
     reach = band // 2 * tile
     span = 3 * rows
 
     def annotate(start, slot):
         at = pl.ds(pl.multiple_of(start, wide), wide)
         first = (lax.axis_index("snp") - 2 + slot) * rows
-        local = idx[:, at] - first
-        strength = lw[:, at]
-        gene = lax.broadcasted_iota(jnp.int32, (span, wide), 0)
-        mix = jnp.zeros((span, wide), F32)
-        for link in range(idx.shape[0]):
-            mix = jnp.where(
-                local[link : link + 1] == gene, strength[link : link + 1], mix
-            )
         ann[:, at] = jnp.dot(
             table[:, slot * rows : slot * rows + span],
-            mix.astype(BF16),
+            one_hot(idx[:, at] - first, lw[:, at], span),
             preferred_element_type=F32,
         ).astype(BF16)
 
@@ -288,9 +299,13 @@
             annotate(start, 0)
             annotate(ann.shape[1] - reach + start, 2)
 
-        @pl.loop(reach // wide, chunks - reach // wide)
+        @pl.loop(0, mix.shape[1] // wide)
         def _(c):
-            annotate(c * wide, 1)
+            ann[:, pl.ds(pl.multiple_of(c * wide + reach, wide), wide)] = jnp.dot(
+                table[:, rows : 4 * rows],
+                mix[:, pl.ds(pl.multiple_of(c * wide, wide), wide)],
+                preferred_element_type=F32,
+            ).astype(BF16)
 
     blocks = []
     for g in range(group):
@@ -309,6 +324,9 @@
     part = sum(part[:, a : a + 128] for a in range(0, wide, 128))
     j = jk_ref[0, unit]
     square[j] += part
+    line = lax.broadcasted_iota(jnp.int32, mask.shape, 0)
+    mine = (line == 0) & (j == 0) | (line == 1) & (j == JK_DEV - 1)
+    mask[...] = jnp.where(mine, 1.0, 0.0).astype(BF16)
 
     @pl.when(unit == pl.num_programs(0) - 1)
     def _():
@@ -333,7 +351,7 @@
     chunks = ROW_CHUNKS
     rows = w_ref.shape[0] // chunks
     half = rows // 2
-    own = half // chips
+    stages = chips.bit_length() - 1
     half_s = w_ref.shape[1] // 2
 
     barrier = pltpu.get_barrier_semaphore()
@@ -353,23 +371,34 @@
     def core_copy(k):
         return remote(c_out.at[k], c_in.at[k], cs.at[k], cr.at[k], mate)
 
-    def peer_copy(k, o):
-        owner = (m + o) % chips
+    sides, mates, offsets = [], [], [0]
+    for t in range(stages):
+        low, high = 2**t, 2 ** (stages - 1 - t)
+        side = (1 - c) * (m // low % 2) + c * (m // high % 2)
+        weight = (1 - c) * low + c * high
+        sides.append(side)
+        mates.append((m + weight * (1 - 2 * side)) * 2 + c)
+        offsets.append(offsets[t] + side * (half >> (t + 1)))
+
+    def part(base, size):
+        return pl.ds(pl.multiple_of(base, size), size)
+
+    def peer_copy(k, t):
+        size = half >> (t + 1)
         return remote(
-            p_out.at[k, pl.ds(pl.multiple_of(owner * own, own), own)],
-            p_in.at[k, o - 1], ps.at[k, o - 1], pr.at[k, o - 1], owner * 2 + c,
-        )
-
-    def place(k, core, chip):
-        return pl.ds(pl.multiple_of(k * rows + core * half + chip * own, own), own)
-
-    def gather_copy(k, o):
-        at = total.at[place(k, c, m)]
-        return remote(at, at, gs.at[k, o - 1], gr.at[k, o - 1], (m + o) % chips * 2 + c)
-
-    def gather_arrive(k, o):
-        at = total.at[place(k, c, (m + chips - o) % chips)]
-        return remote(at, at, gs.at[k, o - 1], gr.at[k, o - 1], mate)
+            p_out.at[k, part(offsets[t] + (1 - sides[t]) * size, size)],
+            p_in.at[k, pl.ds(half - 2 * size, size)], ps.at[k, t], pr.at[k, t], mates[t],
+        )
+
+    def gather_copy(k, t):
+        size = half >> (t + 1)
+        at = total.at[part(k * rows + c * half + offsets[t + 1], size)]
+        return remote(at, at, gs.at[k, t], gr.at[k, t], mates[t])
+
+    def gather_arrive(k, t):
+        size = half >> (t + 1)
+        at = total.at[part(k * rows + c * half + offsets[t] + (1 - sides[t]) * size, size)]
+        return remote(at, at, gs.at[k, t], gr.at[k, t], mates[t])
 
     def half_copy(k, core):
         at = total.at[pl.ds(pl.multiple_of(k * rows + core * half, half), half)]
@@ -385,23 +414,26 @@
         core_copy(k).wait_recv()
         home = pl.ds(pl.multiple_of(k * rows + c * half, half), half)
         p_out[k] = (acc[home, :] + c_in[k].astype(F32)).astype(BF16)
-        for o in range(1, chips):
-            peer_copy(k, o).start()
-
-    def after_peers(k):
-        for o in range(1, chips):
-            peer_copy(k, o).wait_recv()
-        s = p_out[k, pl.ds(pl.multiple_of(m * own, own), own)].astype(F32)
-        for o in range(1, chips):
-            s = s + p_in[k, o - 1].astype(F32)
-        total[place(k, c, m), :] = s.astype(BF16)
-        for o in range(1, chips):
-            gather_copy(k, o).start()
-
-    def after_gather(k):
-        for o in range(1, chips):
-            gather_arrive(k, o).wait_recv()
-        half_copy(k, c).start()
+        peer_copy(k, 0).start()
+
+    def after_peer(k, t):
+        size = half >> (t + 1)
+        peer_copy(k, t).wait_recv()
+        at = part(offsets[t + 1], size)
+        s = p_out[k, at].astype(F32) + p_in[k, half - 2 * size : half - size].astype(F32)
+        if t + 1 < stages:
+            p_out[k, at] = s.astype(BF16)
+            peer_copy(k, t + 1).start()
+        else:
+            total[part(k * rows + c * half + offsets[t + 1], size), :] = s.astype(BF16)
+            gather_copy(k, t).start()
+
+    def after_gather(k, t):
+        gather_arrive(k, t).wait_recv()
+        if t:
+            gather_copy(k, t - 1).start()
+        else:
+            half_copy(k, c).start()
 
     def split(k):
         at = slice(k * rows, (k + 1) * rows)
@@ -422,18 +454,18 @@
     core_copy(0).start()
     for o in range(1, n):
         sq_copy(o).start()
-    for k in range(1, chunks):
-        compute(k)
-        core_copy(k).start()
-        after_core(k - 1)
-    split(0)
-    after_core(chunks - 1)
-    after_peers(0)
-    for k in range(1, chunks):
-        split(k)
-        after_peers(k)
-        after_gather(k - 1)
-    after_gather(chunks - 1)
+    steps = [after_core]
+    steps += [functools.partial(after_peer, t=t) for t in range(stages)]
+    steps += [functools.partial(after_gather, t=t) for t in reversed(range(stages))]
+    for slot in range(max(2 * chunks - 1, chunks + len(steps) - 1)):
+        if slot < chunks - 1:
+            compute(slot + 1)
+            core_copy(slot + 1).start()
+        elif slot < 2 * chunks - 1:
+            split(slot + 1 - chunks)
+        for k in range(chunks):
+            if 0 <= slot - k < len(steps):
+                steps[slot - k](k)
     s = q_out[...]
     for o in range(1, n):
         sq_copy(o).wait_recv()
@@ -445,17 +477,26 @@
         half_copy(k, 1 - c).wait_recv()
         half_copy(k, c).wait_send()
         core_copy(k).wait_send()
-        for o in range(1, chips):
-            peer_copy(k, o).wait_send()
-            gather_copy(k, o).wait_send()
-
-
-def estimate_kernel(crossed, total, leave, keep, delete_one, own):
+        for t in range(stages):
+            peer_copy(k, t).wait_send()
+            gather_copy(k, t).wait_send()
+
+
+def estimate_kernel(crossed, total, sq, sq_total, delete_one, own):
+    block, traits = total.shape
+    line = pl.ds(pl.program_id(0), 1)
     whole = total[...].astype(F32)
+
+    def column(row):
+        turned = jnp.broadcast_to(1.0 / jnp.sqrt(row), (block, block)).T
+        return jnp.concatenate([turned] * (traits // block), axis=1)
+
     for j in range(JK_DEV):
         part = crossed[j].astype(F32)
-        delete_one[j] = ((whole - part) * leave[j]).astype(BF16)
-        own[j] = (part * keep[j]).astype(BF16)
+        row = sq[j, line, :]
+        leave = column(sq_total[line, :] - row)
+        delete_one[j] = ((whole - part) * leave).astype(BF16)
+        own[j] = (part * column(row)).astype(BF16)
 
 
 def on_device(
@@ -475,33 +516,36 @@
     dma = pltpu.SemaphoreType.DMA
     limit = 60 * 1024 * 1024
 
-    table, idx, lw = pl.pallas_call(
-        functools.partial(gather_kernel, n, zn, reach),
+    table, idx, lw, mix = pl.pallas_call(
+        functools.partial(gather_kernel, n, zn, reach, wide),
         out_shape=(
             jax.ShapeDtypeStruct((programs, 5 * rows), BF16),
             jax.ShapeDtypeStruct((links, snps + 2 * reach), jnp.int32),
             jax.ShapeDtypeStruct((links, snps + 2 * reach), F32),
+            jax.ShapeDtypeStruct((3 * rows, snps), BF16),
         ),
         in_specs=[vmem] * 3,
-        out_specs=(vmem,) * 3,
+        out_specs=(vmem,) * 4,
         scratch_shapes=[
             dma((zn - 1,)), dma((zn - 1,)), dma((3, zn)), dma((3, zn)),
             dma((zn,)), dma((zn,)), dma((2, 2)), dma((2, 2)),
         ],
         compiler_params=pltpu.CompilerParams(collective_id=0, has_side_effects=True),
         name="gather_genes",
-    )(gene_score, link_gene.T, link_weight.T.astype(F32))
-
-    weighted, square = pl.pallas_call(
+    )(gene_score, link_gene.T, link_weight.T)
+
+    weighted, square, mask = pl.pallas_call(
         functools.partial(score_kernel, band),
         grid=(unit_count,),
         out_shape=(
             jax.ShapeDtypeStruct((programs, snps), BF16),
             jax.ShapeDtypeStruct((JK_DEV, programs // 128, 128), F32),
+            jax.ShapeDtypeStruct((16, snps), BF16),
         ),
         in_specs=[
             smem,
             smem,
+            vmem,
             vmem,
             vmem,
             vmem,
@@ -511,6 +555,7 @@
         out_specs=(
             pl.BlockSpec((programs, wide), lambda u: (0, u)),
             pl.BlockSpec((JK_DEV, programs // 128, 128), lambda u: (0, 0, 0)),
+            pl.BlockSpec((16, wide), lambda u: (0, u)),
         ),
         scratch_shapes=[
             pltpu.VMEM((programs, snps + 2 * reach), BF16),
@@ -518,15 +563,11 @@
         ],
         compiler_params=pltpu.CompilerParams(vmem_limit_bytes=limit),
         name="ld_scores",
-    )(jk_unit, ld_scale, table, idx, lw, ld_levels, snp_weight[None])
-
-    ends = jnp.array([0, JK_DEV - 1], jnp.int32)
-    mask = jnp.repeat(jk_unit[0][None] == ends[:, None], wide, axis=1).astype(BF16)
-    mask = jnp.pad(mask, ((0, 14), (0, 0)))
+    )(jk_unit, ld_scale, table, idx, lw, mix, ld_levels, snp_weight[None])
 
     k = ROW_CHUNKS
     half = programs // k // 2
-    chips = n // 2
+    stages = (n // 2).bit_length() - 1
     crossed, total, sq_total = pl.pallas_call(
         functools.partial(cross_kernel, n),
         out_shape=(
@@ -541,12 +582,12 @@
             pltpu.VMEM((k, half, traits), BF16),
             pltpu.VMEM((k, half, traits), BF16),
             pltpu.VMEM((k, half, traits), BF16),
-            pltpu.VMEM((k, chips - 1, half // chips, traits), BF16),
+            pltpu.VMEM((k, half, traits), BF16),
             pltpu.VMEM((programs // 128, 128), F32),
             pltpu.VMEM((n - 1, programs // 128, 128), F32),
             dma((k,)), dma((k,)),
-            dma((k, chips - 1)), dma((k, chips - 1)),
-            dma((k, chips - 1)), dma((k, chips - 1)),
+            dma((k, stages)), dma((k, stages)),
+            dma((k, stages)), dma((k, stages)),
             dma((k,)), dma((k,)),
             dma((n - 1,)), dma((n - 1,)),
         ],
@@ -556,20 +597,17 @@
         name="cross_total",
     )(weighted, trait_z, mask, square)
 
-    keep = (1.0 / jnp.sqrt(square)).reshape(JK_DEV, programs, 1)
-    leave = (1.0 / jnp.sqrt(sq_total[None] - square)).reshape(JK_DEV, programs, 1)
-    block = programs // 8
+    block = 128
     whole = pl.BlockSpec((JK_DEV, block, traits), lambda p: (0, p, 0))
-    column = pl.BlockSpec((JK_DEV, block, 1), lambda p: (0, p, 0))
     return pl.pallas_call(
         estimate_kernel,
         grid=(programs // block,),
         out_shape=(jax.ShapeDtypeStruct((JK_DEV, programs, traits), BF16),) * 2,
-        in_specs=[whole, pl.BlockSpec((block, traits), lambda p: (p, 0)), column, column],
+        in_specs=[whole, pl.BlockSpec((block, traits), lambda p: (p, 0)), vmem, vmem],
         out_specs=(whole, whole),
         compiler_params=pltpu.CompilerParams(vmem_limit_bytes=limit),
         name="estimates",
-    )(crossed, total, leave, keep)
+    )(crossed, total, square, sq_total)
 
 
 def solution(mesh):

time: 109 us -> 101 us (0.927)
  local copies, waits for them, and re-layouts: 7.3 us -> 1.36 us
  other arithmetic: 2.87 us -> 0 us
  Pallas kernels: 97.1 us -> 98.5 us
    reshape x2 -> x0, local copies, waits for them, and re-layouts: 5.19 us -> none  [the longest x1 2.64 us: on_device(): (1.0 / jnp.sqrt(sq_total[None] - square)).reshape(JK_DEV, programs, 1)]
    pallas_call x1, Pallas kernels: 39.8 us -> 44.3 us  [on_device(): pl.pallas_call(functools.partial(cross_kernel, n), out_shape=(jax.ShapeDt...]
    pallas_call x1, Pallas kernels: 23.9 us -> 21.4 us  [on_device(): pl.pallas_call(functools.partial(score_kernel, band), grid=(unit_count,),...]
    convert_element_type x2 -> x0, other arithmetic: 2.17 us -> none  [the longest x1 1.45 us: on_device(): link_weight.T.astype(F32)]
    pallas_call x1, Pallas kernels: 11.7 us -> 10.5 us  [on_device(): pl.pallas_call(estimate_kernel, grid=(programs // block,), out_shape=(jax...]
where the time goes in v2:
time: 101 us
  Pallas kernels  98.5 us (98%)
  local copies, waits for them, and re-layouts  1.36 us (1%)
    pallas_call x1, Pallas kernels, on_device(): pl.pallas_call(functools.partial(cross_kernel, n), out_shape=(jax.ShapeDt...  44.3 us
    pallas_call x1, Pallas kernels, on_device(): pl.pallas_call(functools.partial(gather_kernel, n, zn, reach, wide), out_...  22.3 us
    pallas_call x1, Pallas kernels, on_device(): pl.pallas_call(functools.partial(score_kernel, band), grid=(unit_count,),...  21.4 us
    pallas_call x1, Pallas kernels, on_device(): pl.pallas_call(estimate_kernel, grid=(programs // block,), out_shape=(jax...  10.5 us

profile of v2, /device:TPU:0, one launch (start us, length us, event | category | flops | bytes accessed | tf_op | source)
XLA Modules:
  0.0 100.5 jit_solution(5090246472127025957)
XLA Ops:
  0.6 1.4 %copy.10.scale_ref = f32[24,5]{1,0:T(8,128)} copy(f32[24,5]{0,1:T(8,128)} %param.12) | data formatting | bytes 960 | tf_op args[4]
  2.0 22.3 %gather_genes.1 = (bf16[1024,640]{1,0:T(8,128)(2,1)}, s32[8,3584]{1,0:T(8,128)}, f32[8,3584]{1,0:T(8,128)}, bf16[384,3072]{1,0:T(8,128)(2,1)}) custom-call(bf16[128,256]{1,0:T(8,128)(2,1)} %gene_ref.1, s32[8,3072]{1,0:T(8,128)} %bitcast.3, bf16[8,3072]{1,0:T(8,128)(2,1)} %bitcast.4), custom_call_target="tpu_custom_call" | custom-call | tf_op jit(solution)/shard_map/gather_genes/pallas_call | solution.py:519
  24.3 21.4 %ld_scores.1 = (bf16[1024,3072]{1,0:T(8,128)(2,1)}, f32[3,8,128]{2,1,0:T(8,128)}, bf16[16,3072]{1,0:T(8,128)(2,1)}) custom-call(s32[1,12]{1,0:T(1,128)} %jk_ref.1, f32[24,5]{1,0:T(8,128)} %copy.10.scale_ref, bf16[1024,640]{1,0:T(8,128)(2,1)} %get-tuple-element.12.table, s32[8,3584]{1,0:T(8,128)} %get-tuple-element.13.idx, f32[8,3584]{1,0:T(8,128)} %get-tuple-element.14.lw, ...), custom_call_target="tpu_custom_call" | custom-call | tf_op jit(solution)/shard_map/ld_scores/pallas_call | solution.py:537
  45.7 44.3 %cross_total.1 = (bf16[3,1024,1024]{2,1,0:T(8,128)(2,1)}, bf16[1024,1024]{1,0:T(8,128)(2,1)}, f32[8,128]{1,0:T(8,128)}) custom-call(bf16[1024,3072]{1,0:T(8,128)(2,1)} %get-tuple-element.16.w_ref, bf16[3072,1024]{1,0:T(8,128)(2,1)} %z_ref.1, bf16[16,3072]{1,0:T(8,128)(2,1)} %get-tuple-element.17.mask_ref, f32[3,8,128]{2,1,0:T(8,128)} %get-tuple-element.18.sq_ref.sq), custom_call_target="tpu_custom_call" | custom-call | tf_op jit(solution)/shard_map/cross_total/pallas_call | solution.py:571
  90.0 10.5 %estimates.1 = (bf16[3,1024,1024]{2,1,0:T(8,128)(2,1)}, bf16[3,1024,1024]{2,1,0:T(8,128)(2,1)}) custom-call(bf16[3,1024,1024]{2,1,0:T(8,128)(2,1)} %get-tuple-element.19.crossed, bf16[1024,1024]{1,0:T(8,128)(2,1)} %get-tuple-element.20.total, f32[3,8,128]{2,1,0:T(8,128)} %get-tuple-element.18.sq_ref.sq, f32[8,128]{1,0:T(8,128)} %get-tuple-element.21.sq_total), custom_call_target="tpu_custom_call" | custom-call | tf_op jit(solution)/shard_map/estimates/pallas_call | solution.py:602
